TPU v7x, 32 devices: a whole 2x2x4 slice. The times are simulated.
32 devices in a mesh: inst: 8 (over z, y), tp: 4 (over x, core).
Axes of the slice: x: 2, y: 2, z: 4, core: 2. Of those that a mesh axis runs over, the one named last changes fastest.
Arguments:
- queries: bfloat16 [2, 768, 64, 128], P(None, 'inst', 'tp'), may hold values from -8 to 50
- row_prompt: int32 [768], P('inst'), may hold values from 0 to 11, as said below
- owner_slot: int32 [12], replicated, may hold values from 0 to 15, as said below
- suffix_len: int32 [768], P('inst'), may hold values from 1 to 8
- prefix_keys: bfloat16 [16, 4096, 8, 128], P('inst', None, 'tp'), may hold values from -4.5 to 50, as said below
- prefix_values: bfloat16 [16, 4096, 8, 128], P('inst', None, 'tp'), may hold values from -8 to 8, as said below
- suffix_keys: bfloat16 [768, 8, 8, 128], P('inst', None, 'tp'), may hold values from -12 to 12, as said below
- suffix_values: bfloat16 [768, 8, 8, 128], P('inst', None, 'tp'), may hold values from -8 to 8, as said below
- new_keys: bfloat16 [2, 768, 8, 128], P(None, 'inst', 'tp'), may hold values from -12 to 12, as said below
- new_values: bfloat16 [2, 768, 8, 128], P(None, 'inst', 'tp'), may hold values from -8 to 8, as said below
- out_weight: bfloat16 [8192, 2560], P('tp'), may hold values from -0.0625 to 0.0625
Outputs:
- projected: bfloat16 [768, 2, 2560], P(('inst', 'tp'))
Inputs may be any that keep to these rules, and one draw needn't show every extreme that they name: `row_prompt`: samples come in consecutive blocks of 64, one prompt each, every prompt in exactly one block. `owner_slot`: different prompts have different slots. `prefix_keys`: copies of one key-value head are equal. `prefix_values`: copies of one key-value head are equal. `suffix_keys`: copies of one key-value head are equal. `suffix_values`: copies of one key-value head are equal. `new_keys`: copies of one key-value head are equal. `new_values`: copies of one key-value head are equal.
All inputs are finite; a program needn't handle non-finite values.
Results may differ from a plain program's by a relative error of at most 0.0052.
Values may be sent and summed in bfloat16 or wider, within the bound.
No kernel may reach another device: no remote copies, remote signals or barrier semaphores. Data moves between devices by JAX's collectives and lax.ppermute only.
A program may use at most 128 MiB of HBM per device.

v0:
```python
import math

import jax
import jax.numpy as jnp
from jax import lax
from jax.sharding import PartitionSpec as P

GROUP = 64


def prefix_part(query_block, key_block, value_block):
    step_count, row_count, head_count, head_width = query_block.shape
    copy_count = key_block.shape[1]
    grouped = query_block.reshape(
        step_count, row_count, copy_count, head_count // copy_count, head_width
    )
    scores = jnp.einsum(
        "tbcrd,pcd->tbcrp", grouped, key_block, preferred_element_type=jnp.float32
    ) / math.sqrt(head_width)
    highest = jnp.max(scores, axis=-1)
    weights_raw = jnp.exp(scores - highest[..., None])
    weight_sum = jnp.sum(weights_raw, axis=-1)
    summed = jnp.einsum(
        "tbcrp,pcd->tbcrd",
        weights_raw.astype(jnp.bfloat16),
        value_block,
        preferred_element_type=jnp.float32,
    )
    output = (
        (summed / weight_sum[..., None])
        .astype(jnp.bfloat16)
        .reshape(step_count, row_count, head_count, head_width)
    )
    log_total = (highest + jnp.log(weight_sum)).reshape(step_count, row_count, head_count)
    return (output, log_total)


def combine(
    queries, prefix_out, prefix_total, suffix_len, suffix_keys, suffix_values, new_keys, new_values
):
    step_count, row_count, head_count, head_width = queries.shape
    copy_count = suffix_keys.shape[2]
    cache_len = suffix_keys.shape[1]
    all_keys = jnp.concatenate([suffix_keys, jnp.swapaxes(new_keys, 0, 1)], axis=1)
    all_values = jnp.concatenate([suffix_values, jnp.swapaxes(new_values, 0, 1)], axis=1)
    grouped = queries.reshape(
        step_count, row_count, copy_count, head_count // copy_count, head_width
    )
    scores = jnp.einsum(
        "trcxd,rjcd->trcxj", grouped, all_keys, preferred_element_type=jnp.float32
    ) / math.sqrt(head_width)
    key_slots = jnp.arange(cache_len + step_count)
    step_ids = jnp.arange(step_count)
    live = jnp.where(
        key_slots[None, None, :] < cache_len,
        key_slots[None, None, :] < suffix_len[None, :, None],
        key_slots[None, None, :] - cache_len <= step_ids[:, None, None],
    )
    masked = jnp.where(live[:, :, None, None, :], scores, -jnp.inf)
    carried = prefix_total.reshape(step_count, row_count, copy_count, head_count // copy_count)
    highest = jnp.maximum(carried, jnp.max(masked, axis=-1))
    weights_raw = jnp.exp(masked - highest[..., None])
    share = jnp.exp(carried - highest)
    denominator = share + jnp.sum(weights_raw, axis=-1)
    mixed = jnp.einsum(
        "trcxj,rjcd->trcxd",
        weights_raw.astype(jnp.bfloat16),
        all_values,
        preferred_element_type=jnp.float32,
    )
    earlier = prefix_out.reshape(
        step_count, row_count, copy_count, head_count // copy_count, head_width
    ).astype(jnp.float32)
    numerator = share[..., None] * earlier + mixed
    attended = (numerator / denominator[..., None]).astype(jnp.bfloat16)
    return attended.reshape(step_count, row_count, head_count * head_width)


def shards(
    queries,
    row_prompt,
    owner_slot,
    suffix_len,
    prefix_keys,
    prefix_values,
    suffix_keys,
    suffix_values,
    new_keys,
    new_values,
    out_weight,
):
    step_count, local_rows, head_count, head_width = queries.shape
    owned_count = prefix_keys.shape[0]
    inst_index = lax.axis_index("inst")
    row_start = inst_index * local_rows
    global_rows = row_start + jnp.arange(local_rows, dtype=jnp.int32)
    query_all, prompt_all = (
        lax.all_gather(queries, "inst", axis=1, tiled=True),
        lax.all_gather(row_prompt, "inst", axis=0, tiled=True),
    )
    slot_ids = inst_index * owned_count + jnp.arange(owned_count, dtype=jnp.int32)
    matches = owner_slot[None, :] == slot_ids[:, None]
    owned_prompt = jnp.argmax(matches, axis=1)
    first_rows = jnp.argmax(prompt_all[None, :] == owned_prompt[:, None], axis=1)
    outputs = []
    totals = []
    for owned_index in range(owned_count):
        query_block = lax.dynamic_slice_in_dim(query_all, first_rows[owned_index], GROUP, 1)
        part_out, part_total = prefix_part(
            query_block, prefix_keys[owned_index], prefix_values[owned_index]
        )
        outputs.append(part_out)
        totals.append(part_total)
    result_all = lax.all_gather(jnp.stack(outputs), "inst", axis=0, tiled=True)
    total_all = lax.all_gather(jnp.stack(totals), "inst", axis=0, tiled=True)
    row_slot = owner_slot[row_prompt]
    offsets = global_rows % GROUP
    prefix_out = jnp.moveaxis(result_all[row_slot, :, offsets], 0, 1)
    prefix_total = jnp.moveaxis(total_all[row_slot, :, offsets], 0, 1)
    attended = combine(
        queries,
        prefix_out,
        prefix_total,
        suffix_len,
        suffix_keys,
        suffix_values,
        new_keys,
        new_values,
    )
    by_row = jnp.swapaxes(attended, 0, 1)
    summed = lax.psum_scatter(
        jnp.einsum("rtk,kd->rtd", by_row, out_weight, preferred_element_type=jnp.float32),
        "tp",
        scatter_dimension=0,
        tiled=True,
    )
    return summed.astype(jnp.bfloat16)


def solution(mesh):
    placed = (
        P(None, "inst", "tp", None),
        P("inst"),
        P(),
        P("inst"),
        P("inst", None, "tp", None),
        P("inst", None, "tp", None),
        P("inst", None, "tp", None),
        P("inst", None, "tp", None),
        P(None, "inst", "tp", None),
        P(None, "inst", "tp", None),
        P("tp", None),
    )
    return jax.shard_map(
        shards, mesh=mesh, in_specs=placed, out_specs=P(("inst", "tp"), None, None), check_vma=False
    )
```

profile of v0, /device:TPU:0, one launch (start us, length us, event | category | flops | bytes accessed | tf_op | source)
XLA Modules:
  0.0 375.3 jit_solution(6455233426306020218)
XLA Ops:
  6.5 0.7 all-gather.3.cloned.1.call-update
  7.3 1.2 dynamic-slice
  9.2 0.9 dynamic-update-slice
  10.1 13.1 %all-reduce = s32[768]{0:T(1024)S(1)} all-reduce(s32[768]{0:T(1024)S(1)} %dynamic-update-slice), channel_id=1, replica_groups=mesh['inst'=8,'tp'=4] {'inst'}, use_global_device_ids=true, to_apply=%add | all-reduce | flops 768 | bytes 6144
  23.1 1.4 compare_reduce_fusion.1
  29.5 5.8 %fusion.61 = (bf16[1,4096,2,128]{3,2,1,0:T(2,128)(2,1)}, bf16[1,4096,2,128]{3,2,1,0:T(2,128)(2,1)S(1)}) fusion(bf16[2,4096,2,128]{3,2,1,0:T(2,128)(2,1)} %param.15), kind=kLoop, calls=%fused_computation.99 | loop fusion | bytes 8388608 | tf_op jit(solution)/shard_map/slice | solution.py:110
  35.3 4.2 %fusion.62 = (bf16[1,4096,2,128]{3,2,1,0:T(2,128)(2,1)}, bf16[1,4096,2,128]{3,2,1,0:T(2,128)(2,1)}) fusion(bf16[2,4096,2,128]{3,2,1,0:T(2,128)(2,1)S(1)} %copy-done.1), kind=kLoop, calls=%fused_computation.100 | loop fusion | bytes 8388608 | tf_op jit(solution)/shard_map/slice | solution.py:110
  39.5 72.0 %all-gather.3.cloned.1.call-done = bf16[2,768,16,128]{3,2,1,0:T(8,128)(2,1)} async-done(((bf16[2,96,16,128]{3,2,1,0:T(8,128)(2,1)}), bf16[2,768,16,128]{3,2,1,0:T(8,128)(2,1)}) %all-gather.3.cloned.1.call-update) | async-done | bytes 6291472 | tf_op jit(solution)/shard_map/all_gather | solution.py:98
  111.5 1.5 dynamic-slice_bitcast_fusion.1
  113.4 13.1 %bitcast_reduce_fusion.1 = (f32[2,64,2,8]{3,1,0,2:T(8,128)S(1)}, f32[2,2,64,8,4096]{4,3,2,1,0:T(8,128)}) fusion(bf16[1,4096,2,128]{3,2,1,0:T(2,128)(2,1)S(1)} %copy-done, bf16[2,64,2,8,128]{4,3,2,1,0:T(8,128)(2,1)S(1)} %get-tuple-element.11), kind=kOutput, calls=%fused_computation.6 | convolution fusion | flops 2164258816 | bytes 36184064 | tf_op jit(solution)/shard_map/tbcrd,pcd->tbcrp/dot_general | solution.py:17
  126.5 14.0 %fusion.3 = f32[2,64,2,8]{3,1,0,2:T(8,128)S(1)} fusion(f32[2,2,64,8,4096]{4,3,2,1,0:T(8,128)} %get-tuple-element.34, f32[2,64,2,8]{3,1,0,2:T(8,128)S(1)} %get-tuple-element.33), kind=kLoop, calls=%fused_computation.9 | loop fusion | flops 25163776 | bytes 33570816 | tf_op jit(solution)/shard_map/reduce_sum | solution.py:22
  140.5 13.8 %fusion.33 = bf16[2,64,2,8,128]{4,3,1,0,2:T(8,128)(2,1)S(1)} fusion(bf16[1,4096,2,128]{3,2,1,0:T(2,128)(2,1)} %get-tuple-element.15, f32[2,2,64,8,4096]{4,3,2,1,0:T(8,128)} %get-tuple-element.34, f32[2,64,2,8]{3,1,0,2:T(8,128)S(1)} %get-tuple-element.33, f32[2,64,2,8]{3,1,0,2:T(8,128)S(1)} %fusion.3), kind=kOutput, calls=%fused_computation.36 | convolution fusion | flops 2173173760 | bytes 36192256 | tf_op jit(solution)/shard_map/tbcrp,pcd->tbcrd/dot_general | solution.py:23
  154.3 13.1 %bitcast_reduce_fusion = (f32[2,64,2,8]{3,1,0,2:T(8,128)S(1)}, f32[2,2,64,8,4096]{4,3,2,1,0:T(8,128)}) fusion(bf16[1,4096,2,128]{3,2,1,0:T(2,128)(2,1)S(1)} %get-tuple-element.14, bf16[2,64,2,8,128]{4,3,2,1,0:T(8,128)(2,1)S(1)} %get-tuple-element.12), kind=kOutput, calls=%fused_computation.3 | convolution fusion | flops 2164258816 | bytes 36184064 | tf_op jit(solution)/shard_map/tbcrd,pcd->tbcrp/dot_general | solution.py:17
  167.4 14.2 %fusion.5 = f32[2,64,2,8]{3,1,0,2:T(8,128)S(1)} fusion(f32[2,2,64,8,4096]{4,3,2,1,0:T(8,128)} %get-tuple-element.32, f32[2,64,2,8]{3,1,0,2:T(8,128)S(1)} %get-tuple-element.31), kind=kLoop, calls=%fused_computation.11 | loop fusion | flops 25163776 | bytes 33570816 | tf_op jit(solution)/shard_map/reduce_sum | solution.py:22
  181.6 14.1 %fusion.27 = bf16[2,64,2,8,128]{4,3,1,0,2:T(8,128)(2,1)} fusion(bf16[1,4096,2,128]{3,2,1,0:T(2,128)(2,1)S(1)} %copy-done.2, f32[2,2,64,8,4096]{4,3,2,1,0:T(8,128)} %get-tuple-element.32, f32[2,64,2,8]{3,1,0,2:T(8,128)S(1)} %get-tuple-element.31, f32[2,64,2,8]{3,1,0,2:T(8,128)S(1)} %fusion.5), kind=kOutput, calls=%fused_computation.34 | convolution fusion | flops 2173173760 | bytes 36192256 | tf_op jit(solution)/shard_map/tbcrp,pcd->tbcrd/dot_general | solution.py:23
  195.6 1.2 copy_bitcast_fusion.20
  196.9 1.2 pad_maximum_fusion
  198.6 1.5 fusion.65
  200.1 1.0 copy.130
  201.1 0.8 copy.139
  202.1 0.7 fusion.63
  202.8 7.5 %fusion.54 = s32[96]{0:T(128)S(1)} fusion(s32[96]{0:T(128)S(1)} %copy-done.11, s32[]{:T(128)} %bitcast.15, s32[]{:T(128)} %bitcast.16, s32[]{:T(128)} %bitcast.17, s32[]{:T(128)} %bitcast.18, s32[]{:T(128)} %bitcast.19, s32[]{:T(128)} %bitcast.20, s32[]{:T(128)} %bitcast.21, s32[]{:T(128)} %bitcast.22, s32[]{:T(128)} %bitcast.23, s32[]{:T(128)} %bitcast.24, ...), kind=kLoop, calls=%fused_computation.92 | loop fusion | flops 4608 | bytes 820 | tf_op jit(solution)/shard_map/concatenate | solution.py:119
  210.7 31.8 %all_gather.14 = f32[16,2,64,16]{2,3,1,0:T(8,128)S(1)} all-gather(f32[2,2,64,16]{2,3,1,0:T(8,128)S(1)} %pad_maximum_fusion.1), channel_id=1, replica_groups=mesh['inst'=8,'tp'=4] {'inst'}, dimensions={0}, use_global_device_ids=true | all-gather | bytes 147456 | tf_op jit(solution)/shard_map/all_gather | solution.py:115
  243.1 1.2 gather_fusion
  244.6 1.1 fusion.16
  246.2 77.6 %all-gather.5.cloned.1.call-done = bf16[16,2,64,16,128]{4,3,2,1,0:T(8,128)(2,1)} async-done(((bf16[2,2,64,16,128]{4,3,2,1,0:T(8,128)(2,1)}), bf16[16,2,64,16,128]{4,3,2,1,0:T(8,128)(2,1)}) %all-gather.5.cloned.1.call-update) | async-done | bytes 8388624 | tf_op jit(solution)/shard_map/all_gather | solution.py:114
  323.8 4.6 %gather_fusion.1 = bf16[96,2,16,128]{3,2,1,0:T(8,128)(2,1)S(1)} fusion(bf16[16,2,64,16,128]{4,3,2,1,0:T(8,128)(2,1)} %all-gather.5.cloned.1.call-done, s32[96]{0:T(128)S(1)} %fusion.54), kind=kCustom, calls=%fused_computation.1 | custom fusion | bytes 1573632 | tf_op jit(solution)/shard_map/gather | solution.py:118
  328.3 1.6 fusion.15
  330.4 7.5 %fusion.10 = f32[96,2,2560]{2,0,1:T(8,128)} fusion(bf16[2048,2560]{1,0:T(8,128)(2,1)} %param.21, bf16[2,96,2048]{2,1,0:T(8,128)(2,1)S(1)} %reshape.221), kind=kOutput, calls=%fused_computation.14 | convolution fusion | flops 2013265920 | bytes 13238272 | tf_op jit(solution)/shard_map/rtk,kd->rtd/dot_general | solution.py:132
  337.9 29.0 %reduce-scatter.2.cloned.1.call-done = f32[24,2,2560]{2,0,1:T(8,128)} async-done(((f32[96,2,2560]{2,0,1:T(8,128)}), f32[24,2,2560]{2,0,1:T(8,128)}) %reduce-scatter.2.cloned.1.call-update) | async-done | bytes 491536 | tf_op jit(solution)/shard_map/reduce_scatter | solution.py:131
  366.8 1.1 convert_element_type.39
  367.9 0.9 copy.144
  (57 shorter events, 4.5 us)
Async XLA Ops:
  6.5 104.9 %all-gather.3.cloned.1.call-start = ((), (), s32[]{:S(2)}) async-start(), calls=%async_computation.1 | async-start | bytes 7077888 | tf_op jit(solution)/shard_map/all_gather | solution.py:98
  7.3 316.5 %all-gather.5.cloned.1.call-start = ((), (), s32[]{:S(2)}) async-start(), calls=%async_computation.2 | async-start | bytes 9437184 | tf_op jit(solution)/shard_map/all_gather | solution.py:114
  29.4 5.9 %copy-start.1 = (bf16[2,4096,2,128]{3,2,1,0:T(2,128)(2,1)S(1)}, bf16[2,4096,2,128]{3,2,1,0:T(2,128)(2,1)}, u32[]{:S(2)}) copy-start(bf16[2,4096,2,128]{3,2,1,0:T(2,128)(2,1)} %param.16) | copy-start | bytes 12582916
  111.5 1.9 copy-start
  167.4 14.2 %copy-start.2 = (bf16[1,4096,2,128]{3,2,1,0:T(2,128)(2,1)S(1)}, bf16[1,4096,2,128]{3,2,1,0:T(2,128)(2,1)}, u32[]{:S(2)}) copy-start(bf16[1,4096,2,128]{3,2,1,0:T(2,128)(2,1)} %get-tuple-element.16) | copy-start | bytes 6291460
  196.8 1.3 copy-start.4
  196.9 1.4 copy-start.7
  196.9 1.5 copy-start.10
  196.9 1.7 copy-start.3
  198.1 168.8 %reduce-scatter.2.cloned.1.call-start = ((), (), s32[]{:S(2)}) async-start(), calls=%async_computation.3 | async-start | bytes 2457600 | tf_op jit(solution)/shard_map/reduce_scatter | solution.py:131
  198.2 2.9 copy-start.5
  198.6 3.4 copy-start.8
  198.6 3.5 copy-start.9
  198.6 4.2 %copy-start.11 = (s32[96]{0:T(128)S(1)}, s32[96]{0:T(128)}, u32[]{:S(2)}) copy-start(s32[96]{0:T(128)} %param.12) | copy-start | bytes 1156
  244.6 83.7 %copy-start.6 = (bf16[96,8,2,128]{3,1,2,0:T(8,128)(2,1)S(1)}, bf16[96,8,2,128]{3,1,2,0:T(8,128)(2,1)}, u32[]{:S(2)}) copy-start(bf16[96,8,2,128]{3,1,2,0:T(8,128)(2,1)} %copy.139) | copy-start | bytes 1179652
Sparse Core Ops, SparseCore 0:
  9.5 101.8 all-gather.2
  198.2 125.5 all-gather.4
  338.0 28.7 reduce-scatter.1
where the time goes:
time: 376 us; the launch traced here: 375 us
  waiting for transfers between devices  179 us (48%)
  matrix products  64.6 us (17%)
  blocking collectives  44.9 us (12%)
  other arithmetic  41.3 us (11%)
  local copies, waits for them, and re-layouts  27.4 us (7%)
  between operations  17.7 us (5%)
    all_gather x1, waiting for transfers between devices, shards(): result_all = lax.all_gather(jnp.stack(outputs), 'inst', axis=0, tiled=True)  77.6 us
    all_gather x1, waiting for transfers between devices, shards(): lax.all_gather(queries, 'inst', axis=1, tiled=True)  72 us
    all_gather x1, blocking collectives, shards(): total_all = lax.all_gather(jnp.stack(totals), 'inst', axis=0, tiled=True)  31.8 us
    reduce_scatter x1, waiting for transfers between devices, shards(): lax.psum_scatter(jnp.einsum('rtk,kd->rtd', by_row, out_weight, preferred_...  29 us
    reduce_sum x2, other arithmetic, prefix_part(): weight_sum = jnp.sum(weights_raw, axis=-1)  28.2 us
    dot_general x2, matrix products, prefix_part(): jnp.einsum('tbcrp,pcd->tbcrd', weights_raw.astype(jnp.bfloat16), value_bl...  27.8 us
    dot_general x2, matrix products, prefix_part(): jnp.einsum('tbcrd,pcd->tbcrp', grouped, key_block, preferred_element_type...  26.2 us
    unnamed x1, blocking collectives  13.1 us
  transfers between devices with their start and end apart: 3, of which 3 were waited for; matrix products, arithmetic and copies ran while one was open for 8% of the time, Pallas kernels for 0%

commit v1 on v0

v1 whole, which is shorter than its diff:
```python
import functools
import math

import jax
import jax.numpy as jnp
from jax import lax
from jax.experimental import pallas as pl
from jax.experimental.pallas import tpu as pltpu
from jax.sharding import PartitionSpec as P

GROUP = 64
STAT = 16
LARGE, MIDDLE, SMALL = 121 * 512 * 1024, 55 * 1024 * 1024, 16 * 1024 * 1024
BLOCK = 16
BF16 = jnp.bfloat16
F32 = jnp.float32


def pack_kernel(dims, prompt_ref, slot_ref, query_ref, ready_ref, out_ref):
    chains, units, copies, span, cut, group, unit = dims
    lanes, height, width = out_ref.shape
    rows = copies * span * cut * group
    place = lax.broadcasted_iota(jnp.int32, (STAT, width), 0)
    marks = jnp.zeros((STAT, width), F32)
    for u in range(units):
        marks = jnp.where(place == u, slot_ref[prompt_ref[u * unit]].astype(F32), marks)

    @pl.loop(0, lanes)
    def _(k):
        for n in range(chains):
            for u in range(units):
                tiles = [
                    [query_ref[n * span + t, u * unit + r + k * cut].astype(F32) for r in range(cut)]
                    for t in range(span)
                ]
                block = [
                    tiles[t][r][c * group : (c + 1) * group]
                    for c in range(copies)
                    for t in range(span)
                    for r in range(cut)
                ]
                first = (n * units + u) * rows
                out_ref[k, first : first + rows, :] = jnp.concatenate(block, axis=0).astype(BF16)
        out_ref[k, height - STAT :, :] = marks.astype(BF16)


def pack(row_prompt, owner_slot, queries, dims, lanes, ready):
    chains, units, copies, span, cut, group, _ = dims
    width = queries.shape[3]
    height = chains * units * copies * span * cut * group + STAT
    smem = pl.BlockSpec(memory_space=pltpu.SMEM)
    whole = pl.BlockSpec(memory_space=pltpu.VMEM)
    return pl.pallas_call(
        functools.partial(pack_kernel, dims),
        in_specs=[smem, smem, whole, pl.BlockSpec(memory_space=pltpu.HBM)],
        out_specs=whole,
        out_shape=jax.ShapeDtypeStruct((lanes, height, width), BF16),
        compiler_params=pltpu.CompilerParams(vmem_limit_bytes=LARGE),
        name="pack",
    )(row_prompt, owner_slot, queries, ready)


def split_kernel(step, turn_ref, in_ref, *refs):
    out_ref, token_ref, held = refs[-3:]
    copies, total, width = out_ref.shape

    def body(block, out_block):
        held[...] = block[...].astype(F32)
        for c in range(copies):
            out_block[c] = held[pl.ds(c, step, stride=copies), :].astype(BF16)

    token_ref[...] = jnp.zeros_like(token_ref)

    @pl.when(turn_ref[0] == 1)
    def _():
        taken = pl.BlockSpec((step * copies, width), lambda i: (i, 0))
        given = pl.BlockSpec((copies, step, width), lambda i: (0, i, 0))
        pltpu.emit_pipeline(body, grid=(total // step,), in_specs=[taken], out_specs=[given])(in_ref, out_ref)


def split_heads(turn, cache, before=None):
    slots, prompt, copies, width = cache.shape
    total = slots * prompt
    step = math.gcd(total, 1024)
    far = pl.BlockSpec(memory_space=pltpu.HBM)
    extra = [] if before is None else [before.reshape(copies, total, width)]
    out, token = pl.pallas_call(
        functools.partial(split_kernel, step),
        in_specs=[pl.BlockSpec(memory_space=pltpu.SMEM)] + [far] * (1 + len(extra)),
        out_specs=[far, pl.BlockSpec(memory_space=pltpu.VMEM)],
        out_shape=[jax.ShapeDtypeStruct((copies, total, width), BF16), jax.ShapeDtypeStruct((8, 128), F32)],
        scratch_shapes=[pltpu.VMEM((step * copies, width), F32)],
        input_output_aliases={2: 0} if extra else {},
        compiler_params=pltpu.CompilerParams(vmem_limit_bytes=LARGE),
        cost_estimate=pl.CostEstimate(flops=0, bytes_accessed=4 * cache.size, transcendentals=0),
        name="split_heads",
    )(turn, cache.reshape(total * copies, width), *extra)
    return out.reshape(copies, slots, prompt, width), token


def attention_kernel(copies, tiles, scale, query_ref, key_ref, value_ref, out_ref):
    slot, copy = pl.program_id(0), pl.program_id(1)
    lanes, halves, all_rows, width = query_ref.shape
    rows = all_rows // copies
    piece = halves * rows
    per_tile = lanes // tiles
    count = per_tile * piece
    body = out_ref.shape[1] - STAT
    keys, values = key_ref[0, 0], value_ref[0, 0]
    begin = pl.multiple_of(copy * rows, rows)
    for tile in range(tiles):
        labels = range(tile * per_tile, (tile + 1) * per_tile)
        query = query_ref[labels[0] : labels[0] + per_tile, :, pl.ds(begin, rows), :].reshape(count, width)
        scores = lax.dot_general(query, keys, (((1,), (1,)), ((), ())), preferred_element_type=F32)
        highest = jnp.max(scores, axis=1, keepdims=True)
        raw = jnp.exp2((scores - highest) * (scale * math.log2(math.e)))
        total = jnp.sum(raw, axis=1, keepdims=True)
        mixed = jnp.dot(raw.astype(BF16), values, preferred_element_type=F32)
        out = (mixed / total).astype(BF16)
        turned = jnp.broadcast_to(highest * scale + jnp.log(total), (count, width)).T[:STAT]
        gap = jnp.zeros((STAT, rows), F32)
        for n, k in enumerate(labels):
            parts = []
            for h in range(halves):
                start = pl.multiple_of(slot * (halves * all_rows) + (h * all_rows + copy * rows), rows)
                first = n * piece + h * rows
                out_ref[k, pl.ds(start, rows), :] = out[first : first + rows]
                part = turned[:, first : first + rows]
                parts += [jnp.where(copy == c, part, gap) for c in range(copies)]
            if copies * piece < width:
                parts.append(jnp.zeros((STAT, width - copies * piece), F32))
            line = jnp.concatenate(parts, axis=1)
            first = line.astype(BF16).astype(F32)
            second = (line - first).astype(BF16).astype(F32)
            third = line - first - second
            place = lax.broadcasted_iota(jnp.int32, line.shape, 0) - 3 * slot
            packed = jnp.where(place == 0, first, jnp.where(place == 1, second, jnp.where(place == 2, third, 0.0)))
            before = jnp.where(slot + copy == 0, 0.0, out_ref[k, body:, :].astype(F32))
            out_ref[k, body:, :] = (before + packed).astype(BF16)


def prompt_attention(queries, keys, values):
    lanes, pieces, all_rows, width = queries.shape
    copies, slots, prompt, _ = values.shape
    halves = pieces // slots
    tiles = max(1, lanes * halves * all_rows // copies // 256)
    work = lanes * pieces * all_rows * prompt
    return pl.pallas_call(
        functools.partial(attention_kernel, copies, tiles, 1.0 / math.sqrt(width)),
        grid=(slots, copies),
        in_specs=[pl.BlockSpec((lanes, halves, all_rows, width), lambda s, c: (0, s, 0, 0))]
        + [pl.BlockSpec((1, 1) + x.shape[2:], lambda s, c: (c, s, 0, 0)) for x in (keys, values)],
        out_specs=pl.BlockSpec((lanes, pieces * all_rows + STAT, width), lambda s, c: (0, 0, 0)),
        out_shape=jax.ShapeDtypeStruct((lanes, pieces * all_rows + STAT, width), BF16),
        compiler_params=pltpu.CompilerParams(vmem_limit_bytes=LARGE),
        cost_estimate=pl.CostEstimate(
            flops=4 * work * width, bytes_accessed=4 * slots * prompt * copies * width, transcendentals=work
        ),
        name="prompt_attention",
    )(queries, keys, values)


def scatter(slot_of, in_ref, out_ref, chain, slots, units):
    lanes, pieces, rows, _ = out_ref.shape
    halves = pieces // slots
    out_ref[...] = jnp.zeros_like(out_ref)
    for k in range(lanes):
        for u in range(units):
            slot = slot_of(k, u)
            first = (chain * units + u) * rows
            half = (k * units + u) % halves
            out_ref[slot // slots, slot % slots * halves + half] = in_ref[k, first : first + rows, :]


def first_pick_kernel(slots, units, in_ref, *refs):
    out_ref, marks_ref = refs[-2:]
    marks = [in_ref[k, in_ref.shape[1] - STAT :, :].astype(F32) for k in range(out_ref.shape[0])]

    def slot_of(k, u):
        slot = jnp.max(marks[k][u : u + 1, :]).astype(jnp.int32)
        marks_ref[k, u] = slot
        return slot

    scatter(slot_of, in_ref, out_ref, 0, slots, units)


def next_pick_kernel(slots, units, chain, marks_ref, in_ref, *refs):
    scatter(lambda k, u: marks_ref[k, u], in_ref, refs[-1], chain, slots, units)


def pick(block, marks, chain, pieces, rows, slots, units, *ready):
    lanes, _, width = block.shape
    smem = pl.BlockSpec(memory_space=pltpu.SMEM)
    whole = pl.BlockSpec(memory_space=pltpu.VMEM)
    params = dict(
        compiler_params=pltpu.CompilerParams(vmem_limit_bytes=SMALL),
        cost_estimate=pl.CostEstimate(flops=0, bytes_accessed=4 * lanes * pieces * rows * width, transcendentals=0),
        name="pick",
    )
    out = jax.ShapeDtypeStruct((lanes, pieces, rows, width), BF16)
    if marks is None:
        return pl.pallas_call(
            functools.partial(first_pick_kernel, slots, units),
            in_specs=[whole] + [pl.BlockSpec(memory_space=pltpu.HBM)] * len(ready),
            out_specs=[whole, smem],
            out_shape=[out, jax.ShapeDtypeStruct((lanes, units), jnp.int32)],
            **params,
        )(block, *ready)
    return pl.pallas_call(
        functools.partial(next_pick_kernel, slots, units, chain),
        in_specs=[smem, whole] + [pl.BlockSpec(memory_space=pltpu.HBM)] * len(ready),
        out_specs=whole,
        out_shape=out,
        **params,
    )(marks, block, *ready), marks


def sort_kernel(rows, slots, halves, marks_ref, *refs):
    in_refs, out_ref = refs[:-2], refs[-1]
    chains = len(in_refs)
    lanes, height, width = in_refs[0].shape
    units = (out_ref.shape[1] - STAT) // (rows * chains)
    place = lax.broadcasted_iota(jnp.int32, (STAT, width), 0)
    for k in range(lanes):
        tail = jnp.zeros(place.shape, F32)
        for u in range(units):
            owner, slot, half = marks_ref[k, u] // slots, marks_ref[k, u] % slots, (k * units + u) % halves
            start = pl.multiple_of((slot * halves + half) * rows, rows)
            line = []
            for n, in_ref in enumerate(in_refs):
                first = (n * units + u) * rows
                out_ref[k, first : first + rows, :] = in_ref[owner, pl.ds(start, rows), :]
                part = in_ref[owner, height - STAT :, :].astype(F32)
                line.append(part[:, half * rows : (half + 1) * rows])
            if chains * rows < width:
                line.append(jnp.zeros((STAT, width - chains * rows), F32))
            line = jnp.concatenate(line, axis=1)
            for s in range(slots):
                down = (3 * (u - s)) % STAT
                moved = jnp.concatenate([line[STAT - down :], line[: STAT - down]], axis=0) if down else line
                here = (place >= 3 * u) & (place < 3 * u + 3) & (slot == s)
                tail = jnp.where(here, moved, tail)
        out_ref[k, out_ref.shape[1] - STAT :, :] = tail.astype(BF16)


def sort(marks, blocks, rows, slots, halves, ready):
    lanes, units = marks.shape
    width = blocks[0].shape[2]
    height = len(blocks) * units * rows + STAT
    whole = pl.BlockSpec(memory_space=pltpu.VMEM)
    return pl.pallas_call(
        functools.partial(sort_kernel, rows, slots, halves),
        in_specs=[pl.BlockSpec(memory_space=pltpu.SMEM)]
        + [whole] * len(blocks)
        + [pl.BlockSpec(memory_space=pltpu.HBM)],
        out_specs=whole,
        out_shape=jax.ShapeDtypeStruct((lanes, height, width), BF16),
        compiler_params=pltpu.CompilerParams(vmem_limit_bytes=SMALL),
        cost_estimate=pl.CostEstimate(flops=0, bytes_accessed=4 * lanes * height * width, transcendentals=0),
        name="sort",
    )(marks, *blocks, ready)


def own_body(step, scale, query_ref, keys_ref, values_ref, new_keys_ref, new_values_ref, bias_ref, out_ref, log_ref):
    _, samples, heads, width = query_ref.shape
    copies = new_keys_ref.shape[1] // samples
    count = samples * heads
    query = query_ref[...].reshape(count, width)

    def product(keys):
        return lax.dot_general(query, keys, (((1,), (1,)), ((), ())), preferred_element_type=F32) * scale

    old = product(keys_ref[...])
    new = product(new_keys_ref[...].reshape(-1, width))
    per_old = old.shape[1] // samples

    def ids(shape):
        row, column = (lax.broadcasted_iota(jnp.int32, shape, axis) for axis in (0, 1))
        return row // heads, row % heads // (heads // copies), column

    sample, copy, column = ids(old.shape)
    old = jnp.where((column // per_old == sample) & (column % copies == copy), old + bias_ref[0], -jnp.inf)
    sample, copy, column = ids(new.shape)
    newest = column // (samples * copies)
    fits = (newest <= step) & (column // copies % samples == sample) & (column % copies == copy)
    new = jnp.where(fits, new, -jnp.inf)
    highest = jnp.maximum(jnp.max(old, axis=1, keepdims=True), jnp.max(new, axis=1, keepdims=True))
    old = jnp.exp(old - highest)
    new = jnp.exp(new - highest)
    total = jnp.sum(old, axis=1, keepdims=True) + jnp.sum(new, axis=1, keepdims=True)
    mixed = jnp.dot(old.astype(BF16), values_ref[...], preferred_element_type=F32)
    mixed = mixed + jnp.dot(new.astype(BF16), new_values_ref[...].reshape(-1, width), preferred_element_type=F32)
    out_ref[...] = mixed / total
    log_ref[...] = jnp.broadcast_to(highest + jnp.log(total), (count, width))


def own_kernel(step, block, turn_ref, *refs):
    inputs, (out_ref, log_ref, token_ref) = refs[:6], refs[-3:]
    queries, old_keys, _, new_keys, _, _ = inputs
    steps, samples, heads, width = queries.shape
    per_old, per_new = old_keys.shape[0] // samples, new_keys.shape[1] // samples
    token_ref[...] = jnp.zeros_like(token_ref)

    @pl.when(turn_ref[0] == 1)
    def _():
        old = pl.BlockSpec((block * per_old, width), lambda i: (i, 0))
        new = pl.BlockSpec((steps, block * per_new, width), lambda i: (0, i, 0))
        given = pl.BlockSpec((block * heads, width), lambda i: (i, 0))
        pltpu.emit_pipeline(
            functools.partial(own_body, step, 1.0 / math.sqrt(width)),
            grid=(samples // block,),
            in_specs=[
                pl.BlockSpec((1, block, heads, width), lambda i: (step, i, 0, 0)),
                old,
                old,
                new,
                new,
                pl.BlockSpec((1, 1, block * per_old), lambda i: (i, 0, 0)),
            ],
            out_specs=[given, given],
        )(*inputs, out_ref, log_ref)


def own_inputs(queries, suffix_len, suffix_keys, suffix_values, new_keys, new_values):
    steps, samples, _, width = queries.shape
    cached, copies = suffix_keys.shape[1:3]
    live = jnp.arange(cached)[None, :] < suffix_len[:, None]
    bias = jnp.where(jnp.repeat(live, copies, axis=1), 0.0, -jnp.inf).astype(F32)
    return (
        queries,
        suffix_keys.reshape(samples * cached * copies, width),
        suffix_values.reshape(samples * cached * copies, width),
        new_keys.reshape(steps, samples * copies, width),
        new_values.reshape(steps, samples * copies, width),
        bias.reshape(samples // BLOCK, 1, BLOCK * cached * copies),
    )


def own_part(turn, step, inputs, ready=()):
    _, samples, heads, width = inputs[0].shape
    far = pl.BlockSpec(memory_space=pltpu.HBM)
    given = jax.ShapeDtypeStruct((samples * heads, width), F32)
    return pl.pallas_call(
        functools.partial(own_kernel, step, BLOCK),
        in_specs=[pl.BlockSpec(memory_space=pltpu.SMEM)] + [far] * (len(inputs) + len(ready)),
        out_specs=[far, far, pl.BlockSpec(memory_space=pltpu.VMEM)],
        out_shape=[given, given, jax.ShapeDtypeStruct((8, 128), F32)],
        compiler_params=pltpu.CompilerParams(vmem_limit_bytes=LARGE),
        cost_estimate=pl.CostEstimate(flops=0, bytes_accessed=12 * samples * heads * width, transcendentals=0),
        name="own_attention",
    )(turn, *inputs, *ready)


def finish_kernel(
    dims, mine_ref, final_ref, weight_ref, *refs
):
    chains, units, copies, span, cut, group, unit, height = dims
    own_refs, log_refs = refs[: chains * span], refs[chains * span : 2 * chains * span]
    give_ref, keep_ref, merged, lhs, held, sems = refs[2 * chains * span :]
    lanes, _, width = final_ref.shape
    rows = copies * span * cut * group
    heads = copies * group
    steps = chains * span
    samples = units * unit
    body = chains * units * rows
    step = held.shape[2]
    loads = [
        pltpu.make_async_copy(weight_ref.at[:, i * step : (i + 1) * step], held.at[i], sems.at[i])
        for i in range(held.shape[0])
    ]
    for load in loads:
        load.start()

    @pl.loop(0, lanes)
    def _(k):
        logs = final_ref[k, body:, :].astype(F32)
        for u in range(units):
            line = logs[3 * u : 3 * u + 1] + logs[3 * u + 1 : 3 * u + 2] + logs[3 * u + 2 : 3 * u + 3]
            line = jnp.broadcast_to(line, (width, width)).T
            for n in range(chains):
                first = (n * units + u) * rows
                out = final_ref[k, first : first + rows, :].astype(F32)
                for c in range(copies):
                    for t in range(span):
                        for r in range(cut):
                            at = ((c * span + t) * cut + r) * group
                            step_id = n * span + t
                            own_at = pl.multiple_of((u * unit + r) * heads + c * group + k * (cut * heads), group)
                            to = ((u * unit + r) * steps + step_id) * heads + c * group
                            to = pl.multiple_of(to + k * (cut * steps * heads), group)
                            log = line[n * rows + at : n * rows + at + group]
                            own_log = log_refs[step_id][pl.ds(own_at, group), :]
                            top = jnp.maximum(log, own_log)
                            carried = jnp.exp(log - top)
                            share = jnp.exp(own_log - top)
                            numerator = carried * out[at : at + group] + share * own_refs[step_id][pl.ds(own_at, group), :]
                            merged[pl.ds(to, group), :] = numerator / (carried + share)

    for h in range(heads):
        lhs[:, h * width : (h + 1) * width] = merged[pl.ds(h, steps * samples, stride=heads), :].astype(BF16)
    odd = mine_ref[0] == 1
    blocks = samples // height
    for i, load in enumerate(loads):
        load.wait()
        product = jnp.dot(lhs[...], held[i], preferred_element_type=F32)
        even_rows, odd_rows = (
            jnp.concatenate(
                [product[p * height * steps : (p + 1) * height * steps] for p in range(bit, blocks, 2)], axis=0
            )
            for bit in (0, 1)
        )
        give_ref[:, i * step : (i + 1) * step] = jnp.where(odd, even_rows, odd_rows).astype(BF16)
        keep_ref[:, i * step : (i + 1) * step] = jnp.where(odd, odd_rows, even_rows)


def finish(mine, final, own_outs, own_logs, weight, dims):
    chains, units, copies, span, cut, group, unit, height = dims
    width = final.shape[2]
    steps, samples, heads = chains * span, units * unit, copies * group
    depth, columns = weight.shape
    step = math.gcd(columns, 512)
    whole = pl.BlockSpec(memory_space=pltpu.VMEM)
    half = steps * samples // 2
    return pl.pallas_call(
        functools.partial(finish_kernel, dims),
        in_specs=[pl.BlockSpec(memory_space=pltpu.SMEM), whole, pl.BlockSpec(memory_space=pltpu.HBM)]
        + [whole] * (2 * steps),
        out_specs=[whole, whole],
        out_shape=[jax.ShapeDtypeStruct((half, columns), BF16), jax.ShapeDtypeStruct((half, columns), F32)],
        scratch_shapes=[
            pltpu.VMEM((steps * samples * heads, width), F32),
            pltpu.VMEM((steps * samples, heads * width), BF16),
            pltpu.VMEM((columns // step, depth, step), BF16),
            pltpu.SemaphoreType.DMA((columns // step,)),
        ],
        compiler_params=pltpu.CompilerParams(vmem_limit_bytes=MIDDLE),
        cost_estimate=pl.CostEstimate(
            flops=2 * steps * samples * depth * columns, bytes_accessed=2 * depth * columns, transcendentals=0
        ),
        name="finish",
    )(
        mine,
        final,
        weight,
        *own_outs,
        *own_logs,
    )


def projection_kernel(rows_ref, weight_ref, give_ref, keep_ref):
    product = jnp.dot(rows_ref[...], weight_ref[...], preferred_element_type=F32)
    half = give_ref.shape[0]
    give_ref[...] = product[:half].astype(BF16)
    keep_ref[...] = product[half:]


def projection(rows, weight):
    count, depth = rows.shape
    columns = weight.shape[1]
    step = math.gcd(columns, 512)
    return pl.pallas_call(
        projection_kernel,
        grid=(columns // step,),
        in_specs=[
            pl.BlockSpec((count, depth), lambda i: (0, 0)),
            pl.BlockSpec((depth, step), lambda i: (0, i)),
        ],
        out_specs=[pl.BlockSpec((count // 2, step), lambda i: (0, i))] * 2,
        out_shape=[
            jax.ShapeDtypeStruct((count // 2, columns), BF16),
            jax.ShapeDtypeStruct((count // 2, columns), F32),
        ],
        compiler_params=pltpu.CompilerParams(vmem_limit_bytes=LARGE),
        cost_estimate=pl.CostEstimate(
            flops=2 * count * depth * columns, bytes_accessed=2 * depth * columns, transcendentals=0
        ),
        name="projection",
    )(rows, weight)


def swap(block):
    return lax.all_to_all(block, "inst", split_axis=0, concat_axis=0, tiled=True)


def own_attention(queries, suffix_len, suffix_keys, suffix_values, new_keys, new_values):
    step_count, row_count, copy_count, group, width = queries.shape
    cache_len = suffix_keys.shape[1]
    scale = 1.0 / math.sqrt(width)
    old = jnp.einsum("trcxd,rjcd->trcxj", queries, suffix_keys, preferred_element_type=F32) * scale
    new = jnp.einsum("trcxd,urcd->trcxu", queries, new_keys, preferred_element_type=F32) * scale
    live_old = jnp.arange(cache_len)[None, :] < suffix_len[:, None]
    live_new = jnp.arange(step_count)[None, :] <= jnp.arange(step_count)[:, None]
    old = jnp.where(live_old[None, :, None, None, :], old, -jnp.inf)
    new = jnp.where(live_new[:, None, None, None, :], new, -jnp.inf)
    highest = jnp.maximum(jnp.max(old, axis=-1), jnp.max(new, axis=-1))
    old = jnp.exp(old - highest[..., None])
    new = jnp.exp(new - highest[..., None])
    total = jnp.sum(old, axis=-1) + jnp.sum(new, axis=-1)
    mixed = jnp.einsum(
        "trcxj,rjcd->trcxd", old.astype(BF16), suffix_values, preferred_element_type=F32
    ) + jnp.einsum("trcxu,urcd->trcxd", new.astype(BF16), new_values, preferred_element_type=F32)
    return highest, total, mixed


def add_up(given, total, steps, height, tp_size):
    tp_index = lax.axis_index("tp")
    columns = total.shape[1]
    bit = 1
    while True:
        total = total + lax.ppermute(given, "tp", [(i, i ^ bit) for i in range(tp_size)]).astype(F32)
        bit *= 2
        if bit == tp_size:
            return total.astype(BF16).reshape(height, steps, columns)
        pairs = total.reshape(-1, 2, height * steps, columns)
        mine = (tp_index // bit) % 2 == 1
        given = jnp.where(mine, pairs[:, 0], pairs[:, 1]).astype(BF16).reshape(-1, columns)
        total = jnp.where(mine, pairs[:, 1], pairs[:, 0]).reshape(-1, columns)


def shards(
    inst_size,
    tp_size,
    queries,
    row_prompt,
    owner_slot,
    suffix_len,
    prefix_keys,
    prefix_values,
    suffix_keys,
    suffix_values,
    new_keys,
    new_values,
    out_weight,
):
    step_count, local_rows, head_count, width = queries.shape
    slots, _, copies, _ = prefix_keys.shape
    group = head_count // copies
    unit = math.gcd(GROUP, local_rows)
    units = local_rows // unit
    halves = GROUP // unit
    pieces = slots * halves
    cut = unit // inst_size
    span = 1 if cut * group % 16 == 0 else step_count
    chains = step_count // span
    rows = copies * span * cut * group

    height = local_rows // tp_size
    tiled = group % 8 == 0 and head_count % 16 == 0 and height % 8 == 0

    odd = (lax.axis_index("tp") % 2).astype(jnp.int32).reshape(1)
    always = jnp.ones_like(odd)
    keys, token = split_heads(1 - odd, prefix_keys)

    if tiled:
        dims = (chains, units, copies, span, cut, group, unit)
        message = pack(row_prompt, owner_slot, queries, dims, inst_size, token)
    else:
        by_slice = queries.reshape(chains, span, units, inst_size, cut, copies, group, width)
        message = jnp.transpose(by_slice, (3, 0, 2, 5, 1, 4, 6, 7)).reshape(inst_size, -1, width)
        slot_of_unit = jnp.pad(owner_slot[row_prompt[::unit]].astype(BF16), (0, STAT - units))
        marks = jnp.broadcast_to(slot_of_unit[None, :, None], (inst_size, STAT, width))
        message = jnp.concatenate([message, marks], axis=1)
    there = swap(message)
    keys, keys_token = split_heads(odd, prefix_keys, keys)
    values, values_token = split_heads(always, prefix_values)

    results = []
    marks = None
    for n in range(chains):
        picked, marks = pick(there, marks, n, pieces, rows, slots, units, values_token if n else keys_token)
        results.append(prompt_attention(swap(picked), keys, values))
    backs = [swap(result) for result in results]
    token = keys_token
    if tiled:
        inputs = own_inputs(queries, suffix_len, suffix_keys, suffix_values, new_keys, new_values)
        *own, token = own_part(always, 0, inputs, ready=results)
        owns = [own]
    sorted_back = sort(marks, backs, rows, slots, halves, token)
    final = swap(sorted_back)
    if tiled:
        for step in range(1, step_count):
            owns.append(own_part(always, step, inputs, ready=[sorted_back])[:2])
        own_out, own_log = zip(*owns)
        given, total = finish(odd, final, own_out, own_log, out_weight, dims + (height,))
        return add_up(given, total, step_count, height, tp_size)

    grouped = queries.reshape(step_count, local_rows, copies, group, width)
    own_high, own_total, own_mixed = own_attention(
        grouped, suffix_len, suffix_keys, suffix_values, new_keys, new_values
    )
    body = chains * units * rows
    out = final[:, :body].reshape(inst_size, chains, units, copies, span, cut, group, width)
    parts = final[:, body : body + 3 * units].astype(F32).reshape(inst_size, units, 3, width)
    log = parts[:, :, 0] + parts[:, :, 1] + parts[:, :, 2]
    log = log[:, :, : chains * rows].reshape(inst_size, units, chains, copies, span, cut, group)
    prefix_out = jnp.transpose(out, (1, 4, 2, 0, 5, 3, 6, 7)).reshape(grouped.shape)
    prefix_total = jnp.transpose(log, (2, 4, 1, 0, 5, 3, 6)).reshape(grouped.shape[:-1])
    top = jnp.maximum(prefix_total, own_high)
    carried = jnp.exp(prefix_total - top)
    share = jnp.exp(own_high - top)
    denominator = carried + share * own_total
    numerator = carried[..., None] * prefix_out.astype(F32) + share[..., None] * own_mixed
    merged = (numerator / denominator[..., None]).astype(BF16)
    merged = jnp.swapaxes(merged.reshape(step_count, local_rows, head_count * width), 0, 1)
    pairs = merged.reshape(tp_size // 2, 2, height * step_count, head_count * width)
    mine = lax.axis_index("tp") % 2 == 1
    give = jnp.where(mine, pairs[:, 0], pairs[:, 1])
    keep = jnp.where(mine, pairs[:, 1], pairs[:, 0])
    ordered = jnp.stack([give, keep]).reshape(step_count * local_rows, head_count * width)
    given, total = projection(ordered, out_weight)
    return add_up(given, total, step_count, height, tp_size)


def solution(mesh):
    placed = (
        P(None, "inst", "tp", None),
        P("inst"),
        P(),
        P("inst"),
        P("inst", None, "tp", None),
        P("inst", None, "tp", None),
        P("inst", None, "tp", None),
        P("inst", None, "tp", None),
        P(None, "inst", "tp", None),
        P(None, "inst", "tp", None),
        P("tp", None),
    )
    return jax.shard_map(
        functools.partial(shards, mesh.shape["inst"], mesh.shape["tp"]),
        mesh=mesh,
        in_specs=placed,
        out_specs=P(("inst", "tp"), None, None),
        check_vma=False,
    )
```

time: 376 us -> 148 us (0.39)
  waiting for transfers between devices: 179 us -> 25.8 us
  Pallas kernels: 0 us -> 73.2 us
  matrix products: 64.6 us -> 0 us
  other arithmetic: 41.3 us -> 1.47 us
  blocking collectives: 44.9 us -> 14 us
  starting transfers between devices: 0.08 us -> 28.2 us
  local copies, waits for them, and re-layouts: 27.4 us -> 4.07 us
  between operations: 17.7 us -> 0.14 us
    all_gather x2 -> x0, waiting for transfers between devices: 150 us -> none  [the longest x1 77.6 us: shards(): result_all = lax.all_gather(jnp.stack(outputs), 'inst', axis=0, tiled=True)]
    pallas_call x0 -> x12, Pallas kernels: none -> 73.2 us  [the longest x2 30.6 us: prompt_attention(): pl.pallas_call(functools.partial(attention_kernel, copies, tiles, 1.0 / m...]
    dot_general x7 -> x0, matrix products: 64.6 us -> none  [the longest x2 27.8 us: prefix_part(): jnp.einsum('tbcrp,pcd->tbcrd', weights_raw.astype(jnp.bfloat16), value_bl...]
    all_gather x1 -> x0, blocking collectives: 31.8 us -> none  [shards(): total_all = lax.all_gather(jnp.stack(totals), 'inst', axis=0, tiled=True)]
    reduce_sum x3 -> x0, other arithmetic: 29.3 us -> none  [the longest x2 28.2 us: prefix_part(): weight_sum = jnp.sum(weights_raw, axis=-1)]
    reduce_scatter x1 -> x0, waiting for transfers between devices: 29 us -> none  [shards(): lax.psum_scatter(jnp.einsum('rtk,kd->rtd', by_row, out_weight, preferred_...]
    all_to_all x0 -> x5, starting transfers between devices: none -> 26.5 us  [swap(): lax.all_to_all(block, 'inst', split_axis=0, concat_axis=0, tiled=True)]
    all_to_all x0 -> x5, waiting for transfers between devices: none -> 17.3 us  [swap(): lax.all_to_all(block, 'inst', split_axis=0, concat_axis=0, tiled=True)]
  transfers between devices with their start and end apart: 3 -> 7, of which waited for: 3 -> 5; matrix products, arithmetic and copies ran while one was open for 8% -> 1% of each run, Pallas kernels for 0% -> 35%
where the time goes in v1:
time: 148 us; the launch traced here: 147 us
  Pallas kernels  73.2 us (49%)
  starting transfers between devices  28.2 us (19%)
  waiting for transfers between devices  25.8 us (17%)
  blocking collectives  14 us (9%)
  local copies, waits for them, and re-layouts  4.07 us (3%)
    pallas_call x2, Pallas kernels, prompt_attention(): pl.pallas_call(functools.partial(attention_kernel, copies, tiles, 1.0 / m...  30.6 us
    all_to_all x5, starting transfers between devices, swap(): lax.all_to_all(block, 'inst', split_axis=0, concat_axis=0, tiled=True)  26.5 us
    all_to_all x5, waiting for transfers between devices, swap(): lax.all_to_all(block, 'inst', split_axis=0, concat_axis=0, tiled=True)  17.3 us
    pallas_call x3, Pallas kernels, split_heads(): pl.pallas_call(functools.partial(split_kernel, step), in_specs=[pl.BlockS...  15.7 us
    all_to_all x1, blocking collectives, swap(): lax.all_to_all(block, 'inst', split_axis=0, concat_axis=0, tiled=True)  14 us
    pallas_call x2, Pallas kernels, own_part(): pl.pallas_call(functools.partial(own_kernel, step, BLOCK), in_specs=[pl.B...  12.7 us
    ppermute x2, waiting for transfers between devices, add_up(): lax.ppermute(given, 'tp', [(i, i ^ bit) for i in range(tp_size)])  8.54 us
    pallas_call x1, Pallas kernels, finish(): pl.pallas_call(functools.partial(finish_kernel, dims), in_specs=[pl.Block...  8.21 us
  transfers between devices with their start and end apart: 7, of which 5 were waited for; matrix products, arithmetic and copies ran while one was open for 1% of the time, Pallas kernels for 35%

profile of v1, /device:TPU:0, one launch (start us, length us, event | category | flops | bytes accessed | tf_op | source)
XLA Modules:
  0.0 146.9 jit_solution(8587492590642237335)
XLA Ops:
  0.0 7.6 %split_heads.3 = (bf16[2,8192,128]{2,1,0:T(8,128)(2,1)}, f32[8,128]{1,0:T(8,128)}) custom-call(s32[1]{0:T(128)S(6)} %sub.8.turn_ref, bf16[16384,128]{1,0:T(8,128)(2,1)} %bitcast.16), custom_call_target="tpu_custom_call" | custom-call | bytes 8388608 | tf_op jit(solution)/shard_map/split_heads/pallas_call | solution.py:87
  7.6 2.3 %pack.1 = bf16[8,400,128]{2,1,0:T(8,128)(2,1)} custom-call(s32[96]{0:T(128)} %prompt_ref.1, s32[12]{0:T(128)} %slot_ref.1, bf16[2,96,16,128]{3,2,1,0:T(8,128)(2,1)} %refs_0_.3, f32[8,128]{1,0:T(8,128)} %get-tuple-element.20.ready_ref), custom_call_target="tpu_custom_call" | custom-call | tf_op jit(solution)/shard_map/pack/pallas_call | solution.py:53
  9.9 7.3 %all-to-all-start = ((bf16[8,400,128]{2,1,0:T(8,128)(2,1)}), bf16[8,400,128]{2,1,0:T(8,128)(2,1)S(1)}, u32[]{:S(2)}, u32[]{:S(2)}) async-start(bf16[8,400,128]{2,1,0:T(8,128)(2,1)} %pack.1), calls=%async_computation | async-start | bytes 1638400 | tf_op jit(solution)/shard_map/all_to_all | solution.py:482
  17.2 0.6 split_heads.4
  17.8 7.5 %split_heads.5 = (bf16[2,8192,128]{2,1,0:T(8,128)(2,1)}, f32[8,128]{1,0:T(8,128)}) custom-call(s32[1]{0:T(128)} %constant.36.clone.1.turn_ref, bf16[16384,128]{1,0:T(8,128)(2,1)} %bitcast.20), custom_call_target="tpu_custom_call" | custom-call | bytes 8388608 | tf_op jit(solution)/shard_map/split_heads/pallas_call | solution.py:87
  25.3 5.9 %all-to-all-done.in_ref = bf16[8,400,128]{2,1,0:T(8,128)(2,1)S(1)} async-done(((bf16[8,400,128]{2,1,0:T(8,128)(2,1)}), bf16[8,400,128]{2,1,0:T(8,128)(2,1)S(1)}, u32[]{:S(2)}, u32[]{:S(2)}) %all-to-all-start) | async-done | bytes 819232 | tf_op jit(solution)/shard_map/all_to_all | solution.py:482
  31.2 1.1 pick.2
  32.3 0.7 copy-done.1
  33.0 0.8 pick.3
  33.8 14.0 %all_to_all.30.query_ref = bf16[8,4,64,128]{3,2,1,0:T(8,128)(2,1)} all-to-all(bf16[8,4,64,128]{3,2,1,0:T(8,128)(2,1)S(1)} %pick.3), channel_id=1, replica_groups=mesh['inst'=8,'tp'=4] {'inst'}, dimensions={0} | all-to-all | bytes 1048576 | tf_op jit(solution)/shard_map/all_to_all | solution.py:482
  47.8 3.6 %all-to-all-start.1 = ((bf16[8,4,64,128]{3,2,1,0:T(8,128)(2,1)}), bf16[8,4,64,128]{3,2,1,0:T(8,128)(2,1)S(1)}, u32[]{:S(2)}, u32[]{:S(2)}) async-start(bf16[8,4,64,128]{3,2,1,0:T(8,128)(2,1)} %get-tuple-element.24), calls=%async_computation.1 | async-start | bytes 1048576 | tf_op jit(solution)/shard_map/all_to_all | solution.py:482
  51.4 15.3 %prompt_attention.3.refs_7_ = bf16[8,272,128]{2,1,0:T(8,128)(2,1)} custom-call(bf16[8,4,64,128]{3,2,1,0:T(8,128)(2,1)} %all_to_all.30.query_ref, bf16[2,2,4096,128]{3,2,1,0:T(8,128)(2,1)} %bitcast.21, bf16[2,2,4096,128]{3,2,1,0:T(8,128)(2,1)} %bitcast.31), custom_call_target="tpu_custom_call" | custom-call | flops 4294967296 | bytes 8388608 | tf_op jit(solution)/shard_map/prompt_attention/pallas_call | solution.py:148
  66.7 6.0 %all-to-all-start.4 = ((bf16[8,272,128]{2,1,0:T(8,128)(2,1)}), bf16[8,272,128]{2,1,0:T(8,128)(2,1)S(1)}, u32[]{:S(2)}, u32[]{:S(2)}) async-start(bf16[8,272,128]{2,1,0:T(8,128)(2,1)} %prompt_attention.3.refs_7_), calls=%async_computation.4 | async-start | bytes 1114112 | tf_op jit(solution)/shard_map/all_to_all | solution.py:482
  72.7 15.3 %prompt_attention.2.refs_6_ = bf16[8,272,128]{2,1,0:T(8,128)(2,1)} custom-call(bf16[8,4,64,128]{3,2,1,0:T(8,128)(2,1)} %copy-done.4, bf16[2,2,4096,128]{3,2,1,0:T(8,128)(2,1)} %bitcast.22, bf16[2,2,4096,128]{3,2,1,0:T(8,128)(2,1)} %bitcast.32), custom_call_target="tpu_custom_call" | custom-call | flops 4294967296 | bytes 8388608 | tf_op jit(solution)/shard_map/prompt_attention/pallas_call | solution.py:148
  88.0 6.0 %all-to-all-start.2 = ((bf16[8,272,128]{2,1,0:T(8,128)(2,1)}), bf16[8,272,128]{2,1,0:T(8,128)(2,1)S(1)}, u32[]{:S(2)}, u32[]{:S(2)}) async-start(bf16[8,272,128]{2,1,0:T(8,128)(2,1)} %prompt_attention.2.refs_6_), calls=%async_computation.2 | async-start | bytes 1114112 | tf_op jit(solution)/shard_map/all_to_all | solution.py:482
  94.0 0.1 fusion.2
  94.1 0.2 broadcast_in_dim.15
  94.2 0.9 select_n.61.refs_5_
  95.1 6.3 %own_attention.2 = (f32[1536,128]{1,0:T(8,128)}, f32[1536,128]{1,0:T(8,128)}, f32[8,128]{1,0:T(8,128)}) custom-call(s32[1]{0:T(128)} %constant.36.clone.1.turn_ref, bf16[2,96,16,128]{3,2,1,0:T(8,128)(2,1)} %refs_0_.3, bf16[1536,128]{1,0:T(8,128)(2,1)} %bitcast.23, bf16[1536,128]{1,0:T(8,128)(2,1)} %bitcast.25, bf16[2,192,128]{2,1,0:T(8,128)(2,1)} %bitcast.27, ...), custom_call_target="tpu_custom_call" | custom-call | bytes 2359296 | tf_op jit(solution)/shard_map/own_attention/pallas_call | solution.py:343
  101.4 3.2 %all-to-all-done.2.refs_0_ = bf16[8,272,128]{2,1,0:T(8,128)(2,1)S(1)} async-done(((bf16[8,272,128]{2,1,0:T(8,128)(2,1)}), bf16[8,272,128]{2,1,0:T(8,128)(2,1)S(1)}, u32[]{:S(2)}, u32[]{:S(2)}) %all-to-all-start.2) | async-done | bytes 557088 | tf_op jit(solution)/shard_map/all_to_all | solution.py:482
  104.6 0.7 copy-done.2
  105.3 1.8 %sort.1.refs_6_ = bf16[8,400,128]{2,1,0:T(8,128)(2,1)} custom-call(s32[8,3]{1,0:T(8,128)S(1)} %get-tuple-element.23.marks_ref, bf16[8,272,128]{2,1,0:T(8,128)(2,1)S(1)} %all-to-all-done.2.refs_0_, bf16[8,272,128]{2,1,0:T(8,128)(2,1)S(1)} %all-to-all-done.4.refs_1_, f32[8,128]{1,0:T(8,128)S(1)} %copy-done.2), custom_call_target="tpu_custom_call" | custom-call | bytes 1638400 | tf_op jit(solution)/shard_map/sort/pallas_call | solution.py:251
  107.1 3.7 %all-to-all-start.5 = ((bf16[8,400,128]{2,1,0:T(8,128)(2,1)}), bf16[8,400,128]{2,1,0:T(8,128)(2,1)S(1)}, u32[]{:S(2)}, u32[]{:S(2)}) async-start(bf16[8,400,128]{2,1,0:T(8,128)(2,1)} %sort.1.refs_6_), calls=%async_computation.5 | async-start | bytes 1638400 | tf_op jit(solution)/shard_map/all_to_all | solution.py:482
  110.7 6.4 %own_attention.3 = (f32[1536,128]{1,0:T(8,128)}, f32[1536,128]{1,0:T(8,128)}, f32[8,128]{1,0:T(8,128)}) custom-call(s32[1]{0:T(128)} %constant.36.clone.1.turn_ref, bf16[2,96,16,128]{3,2,1,0:T(8,128)(2,1)} %refs_0_.3, bf16[1536,128]{1,0:T(8,128)(2,1)} %bitcast.24, bf16[1536,128]{1,0:T(8,128)(2,1)} %bitcast.26, bf16[2,192,128]{2,1,0:T(8,128)(2,1)} %bitcast.28, ...), custom_call_target="tpu_custom_call" | custom-call | bytes 2359296 | tf_op jit(solution)/shard_map/own_attention/pallas_call | solution.py:343
  117.1 8.2 %all-to-all-done.5.final_ref = bf16[8,400,128]{2,1,0:T(8,128)(2,1)S(1)} async-done(((bf16[8,400,128]{2,1,0:T(8,128)(2,1)}), bf16[8,400,128]{2,1,0:T(8,128)(2,1)S(1)}, u32[]{:S(2)}, u32[]{:S(2)}) %all-to-all-start.5) | async-done | bytes 819232 | tf_op jit(solution)/shard_map/all_to_all | solution.py:482
  125.3 0.9 copy-done.3
  126.3 8.2 %finish.1 = (bf16[96,2560]{1,0:T(8,128)(2,1)}, f32[96,2560]{1,0:T(8,128)}) custom-call(s32[1]{0:T(128)} %bitcast.turn_ref.mine_ref, bf16[8,400,128]{2,1,0:T(8,128)(2,1)} %copy-done.3, bf16[2048,2560]{1,0:T(8,128)(2,1)} %weight_ref.1, f32[1536,128]{1,0:T(8,128)} %get-tuple-element.29.refs_0_, f32[1536,128]{1,0:T(8,128)} %get-tuple-element.30.refs_1_, ...), custom_call_target="tpu_custom_call" | custom-call | flops 2013265920 | bytes 10485760 | tf_op jit(solution)/shard_map/finish/pallas_call | solution.py:424
  134.6 2.0 %collective-permute-done = bf16[96,2560]{1,0:T(8,128)(2,1)S(1)} collective-permute-done((bf16[96,2560]{1,0:T(8,128)(2,1)}, bf16[96,2560]{1,0:T(8,128)(2,1)S(1)}, u32[]{:S(2)}, u32[]{:S(2)}) %collective-permute-start) | collective-permute-done | bytes 491552 | tf_op jit(solution)/shard_map/ppermute | solution.py:510
  136.6 1.3 convert_add_fusion
  138.0 1.6 %collective-permute-start.1 = (bf16[48,2560]{1,0:T(8,128)(2,1)S(1)}, bf16[48,2560]{1,0:T(8,128)(2,1)S(1)}, u32[]{:S(2)}, u32[]{:S(2)}) collective-permute-start(bf16[48,2560]{1,0:T(8,128)(2,1)S(1)} %fusion.1), channel_id=1, source_target_pairs={{0,2},{1,3},{2,0},{3,1},{4,6},{5,7},{6,4},{7,5},{8,10},{9,11},{10,... | collective-permute-start | bytes 737288 | tf_op jit(solution)/shard_map/ppermute | solution.py:510
  139.5 6.5 %collective-permute-done.1 = bf16[48,2560]{1,0:T(8,128)(2,1)S(1)} collective-permute-done((bf16[48,2560]{1,0:T(8,128)(2,1)S(1)}, bf16[48,2560]{1,0:T(8,128)(2,1)S(1)}, u32[]{:S(2)}, u32[]{:S(2)}) %collective-permute-start.1) | collective-permute-done | bytes 245792 | tf_op jit(solution)/shard_map/ppermute | solution.py:510
  146.1 0.8 reshape.82
  (14 shorter events, 0.2 us)
Async XLA Ops:
  9.9 21.3 %all-to-all-start = ((bf16[8,400,128]{2,1,0:T(8,128)(2,1)}), bf16[8,400,128]{2,1,0:T(8,128)(2,1)S(1)}, u32[]{:S(2)}, u32[]{:S(2)}) async-start(bf16[8,400,128]{2,1,0:T(8,128)(2,1)} %pack.1), calls=%async_computation | async-start | bytes 1638400 | tf_op jit(solution)/shard_map/all_to_all | solution.py:482
  17.8 13.4 %copy-start = (f32[8,128]{1,0:T(8,128)S(1)}, f32[8,128]{1,0:T(8,128)}, u32[]{:S(2)}) copy-start(f32[8,128]{1,0:T(8,128)} %get-tuple-element.22.refs_0_) | copy-start | bytes 12292
  32.3 0.7 copy-start.1
  47.8 18.9 %all-to-all-start.1 = ((bf16[8,4,64,128]{3,2,1,0:T(8,128)(2,1)}), bf16[8,4,64,128]{3,2,1,0:T(8,128)(2,1)S(1)}, u32[]{:S(2)}, u32[]{:S(2)}) async-start(bf16[8,4,64,128]{3,2,1,0:T(8,128)(2,1)} %get-tuple-element.24), calls=%async_computation.1 | async-start | bytes 1048576 | tf_op jit(solution)/shard_map/all_to_all | solution.py:482
  66.7 6.0 %copy-start.4 = (bf16[8,4,64,128]{3,2,1,0:T(8,128)(2,1)}, bf16[8,4,64,128]{3,2,1,0:T(8,128)(2,1)S(1)}, u32[]{:S(2)}) copy-start(bf16[8,4,64,128]{3,2,1,0:T(8,128)(2,1)S(1)} %all-to-all-done.1.query_ref) | copy-start | bytes 1572868
  66.7 21.3 %all-to-all-start.4 = ((bf16[8,272,128]{2,1,0:T(8,128)(2,1)}), bf16[8,272,128]{2,1,0:T(8,128)(2,1)S(1)}, u32[]{:S(2)}, u32[]{:S(2)}) async-start(bf16[8,272,128]{2,1,0:T(8,128)(2,1)} %prompt_attention.3.refs_7_), calls=%async_computation.4 | async-start | bytes 1114112 | tf_op jit(solution)/shard_map/all_to_all | solution.py:482
  72.7 21.3 %copy-start.5 = (s32[96]{0:T(128)S(1)}, s32[96]{0:T(128)}, u32[]{:S(2)}) copy-start(s32[96]{0:T(128)} %param.14) | copy-start | bytes 1156
  88.0 16.6 %all-to-all-start.2 = ((bf16[8,272,128]{2,1,0:T(8,128)(2,1)}), bf16[8,272,128]{2,1,0:T(8,128)(2,1)S(1)}, u32[]{:S(2)}, u32[]{:S(2)}) async-start(bf16[8,272,128]{2,1,0:T(8,128)(2,1)} %prompt_attention.2.refs_6_), calls=%async_computation.2 | async-start | bytes 1114112 | tf_op jit(solution)/shard_map/all_to_all | solution.py:482
  104.6 0.7 copy-start.2
  107.1 18.3 %all-to-all-start.5 = ((bf16[8,400,128]{2,1,0:T(8,128)(2,1)}), bf16[8,400,128]{2,1,0:T(8,128)(2,1)S(1)}, u32[]{:S(2)}, u32[]{:S(2)}) async-start(bf16[8,400,128]{2,1,0:T(8,128)(2,1)} %sort.1.refs_6_), calls=%async_computation.5 | async-start | bytes 1638400 | tf_op jit(solution)/shard_map/all_to_all | solution.py:482
  125.3 0.9 copy-start.3
  134.5 2.1 %collective-permute-start = (bf16[96,2560]{1,0:T(8,128)(2,1)}, bf16[96,2560]{1,0:T(8,128)(2,1)S(1)}, u32[]{:S(2)}, u32[]{:S(2)}) collective-permute-start(bf16[96,2560]{1,0:T(8,128)(2,1)} %get-tuple-element.34), channel_id=1, source_target_pairs={{0,1},{1,0},{2,3},{3,2},{4,5},{5,4},{6,7},{7,6},{8,9},{9,8},{10,11... | collective-permute-start | bytes 1474568 | tf_op jit(solution)/shard_map/ppermute | solution.py:510
  138.0 8.1 %collective-permute-start.1 = (bf16[48,2560]{1,0:T(8,128)(2,1)S(1)}, bf16[48,2560]{1,0:T(8,128)(2,1)S(1)}, u32[]{:S(2)}, u32[]{:S(2)}) collective-permute-start(bf16[48,2560]{1,0:T(8,128)(2,1)S(1)} %fusion.1), channel_id=1, source_target_pairs={{0,2},{1,3},{2,0},{3,1},{4,6},{5,7},{6,4},{7,5},{8,10},{9,11},{10,... | collective-permute-start | bytes 737288 | tf_op jit(solution)/shard_map/ppermute | solution.py:510

commit v2 on v1

--- a/solution.py
+++ b/solution.py
@@ -216,7 +216,7 @@
 
 
 def sort_kernel(rows, slots, halves, marks_ref, *refs):
-    in_refs, out_ref = refs[:-2], refs[-1]
+    in_refs, out_ref = refs[:-1], refs[-1]
     chains = len(in_refs)
     lanes, height, width = in_refs[0].shape
     units = (out_ref.shape[1] - STAT) // (rows * chains)
@@ -243,22 +243,20 @@
         out_ref[k, out_ref.shape[1] - STAT :, :] = tail.astype(BF16)
 
 
-def sort(marks, blocks, rows, slots, halves, ready):
+def sort(marks, blocks, rows, slots, halves):
     lanes, units = marks.shape
     width = blocks[0].shape[2]
     height = len(blocks) * units * rows + STAT
     whole = pl.BlockSpec(memory_space=pltpu.VMEM)
     return pl.pallas_call(
         functools.partial(sort_kernel, rows, slots, halves),
-        in_specs=[pl.BlockSpec(memory_space=pltpu.SMEM)]
-        + [whole] * len(blocks)
-        + [pl.BlockSpec(memory_space=pltpu.HBM)],
+        in_specs=[pl.BlockSpec(memory_space=pltpu.SMEM)] + [whole] * len(blocks),
         out_specs=whole,
         out_shape=jax.ShapeDtypeStruct((lanes, height, width), BF16),
         compiler_params=pltpu.CompilerParams(vmem_limit_bytes=SMALL),
         cost_estimate=pl.CostEstimate(flops=0, bytes_accessed=4 * lanes * height * width, transcendentals=0),
         name="sort",
-    )(marks, *blocks, ready)
+    )(marks, *blocks)
 
 
 def own_body(step, scale, query_ref, keys_ref, values_ref, new_keys_ref, new_values_ref, bias_ref, out_ref, log_ref):
@@ -570,16 +568,11 @@
         picked, marks = pick(there, marks, n, pieces, rows, slots, units, values_token if n else keys_token)
         results.append(prompt_attention(swap(picked), keys, values))
     backs = [swap(result) for result in results]
-    token = keys_token
+    sorted_back = sort(marks, backs, rows, slots, halves)
+    final = swap(sorted_back)
     if tiled:
         inputs = own_inputs(queries, suffix_len, suffix_keys, suffix_values, new_keys, new_values)
-        *own, token = own_part(always, 0, inputs, ready=results)
-        owns = [own]
-    sorted_back = sort(marks, backs, rows, slots, halves, token)
-    final = swap(sorted_back)
-    if tiled:
-        for step in range(1, step_count):
-            owns.append(own_part(always, step, inputs, ready=[sorted_back])[:2])
+        owns = [own_part(always, step, inputs, ready=[sorted_back])[:2] for step in range(step_count)]
         own_out, own_log = zip(*owns)
         given, total = finish(odd, final, own_out, own_log, out_weight, dims + (height,))
         return add_up(given, total, step_count, height, tp_size)

time: 148 us -> 148 us (level)
  blocking collectives: 14 us -> 31.5 us
  waiting for transfers between devices: 25.8 us -> 14.7 us
  starting transfers between devices: 28.2 us -> 22.1 us
    all_to_all x1 -> x2, blocking collectives: 14 us -> 31.5 us  [swap(): lax.all_to_all(block, 'inst', split_axis=0, concat_axis=0, tiled=True)]
    all_to_all x5 -> x4, waiting for transfers between devices: 17.3 us -> 6.24 us  [swap(): lax.all_to_all(block, 'inst', split_axis=0, concat_axis=0, tiled=True)]
    all_to_all x5 -> x4, starting transfers between devices: 26.5 us -> 20.4 us  [swap(): lax.all_to_all(block, 'inst', split_axis=0, concat_axis=0, tiled=True)]
  transfers between devices with their start and end apart: 7 -> 6, of which waited for: 5 -> 4; matrix products, arithmetic and copies ran while one was open for 1% -> 1% of each run, Pallas kernels for 35% -> 35%
where the time goes in v2:
time: 148 us; the launch traced here: 146 us
  Pallas kernels  73.1 us (49%)
  blocking collectives  31.5 us (21%)
  starting transfers between devices  22.1 us (15%)
  waiting for transfers between devices  14.7 us (10%)
  local copies, waits for them, and re-layouts  3.41 us (2%)
    all_to_all x2, blocking collectives, swap(): lax.all_to_all(block, 'inst', split_axis=0, concat_axis=0, tiled=True)  31.5 us
    pallas_call x2, Pallas kernels, prompt_attention(): pl.pallas_call(functools.partial(attention_kernel, copies, tiles, 1.0 / m...  30.6 us
    all_to_all x4, starting transfers between devices, swap(): lax.all_to_all(block, 'inst', split_axis=0, concat_axis=0, tiled=True)  20.4 us
    pallas_call x3, Pallas kernels, split_heads(): pl.pallas_call(functools.partial(split_kernel, step), in_specs=[pl.BlockS...  15.6 us
    pallas_call x2, Pallas kernels, own_part(): pl.pallas_call(functools.partial(own_kernel, step, BLOCK), in_specs=[pl.B...  12.7 us
    ppermute x2, waiting for transfers between devices, add_up(): lax.ppermute(given, 'tp', [(i, i ^ bit) for i in range(tp_size)])  8.44 us
    pallas_call x1, Pallas kernels, finish(): pl.pallas_call(functools.partial(finish_kernel, dims), in_specs=[pl.Block...  8.21 us
    all_to_all x4, waiting for transfers between devices, swap(): lax.all_to_all(block, 'inst', split_axis=0, concat_axis=0, tiled=True)  6.24 us
  transfers between devices with their start and end apart: 6, of which 4 were waited for; matrix products, arithmetic and copies ran while one was open for 1% of the time, Pallas kernels for 35%

profile of v2, /device:TPU:0, one launch (start us, length us, event | category | flops | bytes accessed | tf_op | source)
XLA Modules:
  0.0 146.4 jit_solution(5021510438070302835)
XLA Ops:
  0.0 7.5 %split_heads.3 = (bf16[2,8192,128]{2,1,0:T(8,128)(2,1)}, f32[8,128]{1,0:T(8,128)}) custom-call(s32[1]{0:T(128)S(6)} %sub.8.turn_ref, bf16[16384,128]{1,0:T(8,128)(2,1)} %bitcast.16), custom_call_target="tpu_custom_call" | custom-call | bytes 8388608 | tf_op jit(solution)/shard_map/split_heads/pallas_call | solution.py:87
  7.5 2.3 %pack.1 = bf16[8,400,128]{2,1,0:T(8,128)(2,1)} custom-call(s32[96]{0:T(128)} %prompt_ref.1, s32[12]{0:T(128)} %slot_ref.1, bf16[2,96,16,128]{3,2,1,0:T(8,128)(2,1)} %refs_0_.3, f32[8,128]{1,0:T(8,128)} %get-tuple-element.19.ready_ref), custom_call_target="tpu_custom_call" | custom-call | tf_op jit(solution)/shard_map/pack/pallas_call | solution.py:53
  9.9 7.3 %all-to-all-start = ((bf16[8,400,128]{2,1,0:T(8,128)(2,1)}), bf16[8,400,128]{2,1,0:T(8,128)(2,1)S(1)}, u32[]{:S(2)}, u32[]{:S(2)}) async-start(bf16[8,400,128]{2,1,0:T(8,128)(2,1)} %pack.1), calls=%async_computation | async-start | bytes 1638400 | tf_op jit(solution)/shard_map/all_to_all | solution.py:480
  17.1 0.6 split_heads.4
  17.7 7.5 %split_heads.5 = (bf16[2,8192,128]{2,1,0:T(8,128)(2,1)}, f32[8,128]{1,0:T(8,128)}) custom-call(s32[1]{0:T(128)} %constant.36.clone.1.turn_ref, bf16[16384,128]{1,0:T(8,128)(2,1)} %bitcast.20), custom_call_target="tpu_custom_call" | custom-call | bytes 8388608 | tf_op jit(solution)/shard_map/split_heads/pallas_call | solution.py:87
  25.2 5.9 %all-to-all-done.in_ref = bf16[8,400,128]{2,1,0:T(8,128)(2,1)S(1)} async-done(((bf16[8,400,128]{2,1,0:T(8,128)(2,1)}), bf16[8,400,128]{2,1,0:T(8,128)(2,1)S(1)}, u32[]{:S(2)}, u32[]{:S(2)}) %all-to-all-start) | async-done | bytes 819232 | tf_op jit(solution)/shard_map/all_to_all | solution.py:480
  31.2 1.1 pick.2
  32.3 0.7 copy-done.1
  33.0 0.8 pick.3
  33.8 13.9 %all_to_all.30.query_ref = bf16[8,4,64,128]{3,2,1,0:T(8,128)(2,1)} all-to-all(bf16[8,4,64,128]{3,2,1,0:T(8,128)(2,1)S(1)} %pick.3), channel_id=1, replica_groups=mesh['inst'=8,'tp'=4] {'inst'}, dimensions={0} | all-to-all | bytes 1048576 | tf_op jit(solution)/shard_map/all_to_all | solution.py:480
  47.7 3.6 %all-to-all-start.1 = ((bf16[8,4,64,128]{3,2,1,0:T(8,128)(2,1)}), bf16[8,4,64,128]{3,2,1,0:T(8,128)(2,1)S(1)}, u32[]{:S(2)}, u32[]{:S(2)}) async-start(bf16[8,4,64,128]{3,2,1,0:T(8,128)(2,1)} %get-tuple-element.23), calls=%async_computation.1 | async-start | bytes 1048576 | tf_op jit(solution)/shard_map/all_to_all | solution.py:480
  51.3 15.3 %prompt_attention.3 = bf16[8,272,128]{2,1,0:T(8,128)(2,1)} custom-call(bf16[8,4,64,128]{3,2,1,0:T(8,128)(2,1)} %all_to_all.30.query_ref, bf16[2,2,4096,128]{3,2,1,0:T(8,128)(2,1)} %bitcast.21, bf16[2,2,4096,128]{3,2,1,0:T(8,128)(2,1)} %bitcast.31), custom_call_target="tpu_custom_call" | custom-call | flops 4294967296 | bytes 8388608 | tf_op jit(solution)/shard_map/prompt_attention/pallas_call | solution.py:148
  66.7 6.0 %all-to-all-start.4 = ((bf16[8,272,128]{2,1,0:T(8,128)(2,1)}), bf16[8,272,128]{2,1,0:T(8,128)(2,1)S(1)}, u32[]{:S(2)}, u32[]{:S(2)}) async-start(bf16[8,272,128]{2,1,0:T(8,128)(2,1)} %prompt_attention.3), calls=%async_computation.4 | async-start | bytes 1114112 | tf_op jit(solution)/shard_map/all_to_all | solution.py:480
  72.6 15.3 %prompt_attention.2 = bf16[8,272,128]{2,1,0:T(8,128)(2,1)} custom-call(bf16[8,4,64,128]{3,2,1,0:T(8,128)(2,1)} %copy-done.3, bf16[2,2,4096,128]{3,2,1,0:T(8,128)(2,1)} %bitcast.22, bf16[2,2,4096,128]{3,2,1,0:T(8,128)(2,1)} %bitcast.32), custom_call_target="tpu_custom_call" | custom-call | flops 4294967296 | bytes 8388608 | tf_op jit(solution)/shard_map/prompt_attention/pallas_call | solution.py:148
  87.9 17.5 %all_to_all.31.refs_0_ = bf16[8,272,128]{2,1,0:T(8,128)(2,1)S(1)} all-to-all(bf16[8,272,128]{2,1,0:T(8,128)(2,1)} %prompt_attention.2), channel_id=1, replica_groups=mesh['inst'=8,'tp'=4] {'inst'}, dimensions={0} | all-to-all | bytes 1114112 | tf_op jit(solution)/shard_map/all_to_all | solution.py:480
  105.4 1.8 %sort.1.refs_6_ = bf16[8,400,128]{2,1,0:T(8,128)(2,1)} custom-call(s32[8,3]{1,0:T(8,128)S(1)} %get-tuple-element.22.marks_ref, bf16[8,272,128]{2,1,0:T(8,128)(2,1)S(1)} %all_to_all.31.refs_0_, bf16[8,272,128]{2,1,0:T(8,128)(2,1)S(1)} %all-to-all-done.4.refs_1_), custom_call_target="tpu_custom_call" | custom-call | bytes 1638400 | tf_op jit(solution)/shard_map/sort/pallas_call | solution.py:251
  107.2 3.5 %all-to-all-start.5 = ((bf16[8,400,128]{2,1,0:T(8,128)(2,1)}), bf16[8,400,128]{2,1,0:T(8,128)(2,1)S(1)}, u32[]{:S(2)}, u32[]{:S(2)}) async-start(bf16[8,400,128]{2,1,0:T(8,128)(2,1)} %sort.1.refs_6_), calls=%async_computation.5 | async-start | bytes 1638400 | tf_op jit(solution)/shard_map/all_to_all | solution.py:480
  110.8 0.1 fusion.2
  110.9 0.2 broadcast_in_dim.15
  111.0 0.9 select_n.61.refs_5_
  111.9 6.3 %own_attention.2 = (f32[1536,128]{1,0:T(8,128)}, f32[1536,128]{1,0:T(8,128)}, f32[8,128]{1,0:T(8,128)}) custom-call(s32[1]{0:T(128)} %constant.36.clone.1.turn_ref, bf16[2,96,16,128]{3,2,1,0:T(8,128)(2,1)} %refs_0_.3, bf16[1536,128]{1,0:T(8,128)(2,1)} %bitcast.23, bf16[1536,128]{1,0:T(8,128)(2,1)} %bitcast.25, bf16[2,192,128]{2,1,0:T(8,128)(2,1)} %bitcast.27, ...), custom_call_target="tpu_custom_call" | custom-call | bytes 2359296 | tf_op jit(solution)/shard_map/own_attention/pallas_call | solution.py:341
  118.2 6.4 %own_attention.3 = (f32[1536,128]{1,0:T(8,128)}, f32[1536,128]{1,0:T(8,128)}, f32[8,128]{1,0:T(8,128)}) custom-call(s32[1]{0:T(128)} %constant.36.clone.1.turn_ref, bf16[2,96,16,128]{3,2,1,0:T(8,128)(2,1)} %refs_0_.3, bf16[1536,128]{1,0:T(8,128)(2,1)} %bitcast.24, bf16[1536,128]{1,0:T(8,128)(2,1)} %bitcast.26, bf16[2,192,128]{2,1,0:T(8,128)(2,1)} %bitcast.28, ...), custom_call_target="tpu_custom_call" | custom-call | bytes 2359296 | tf_op jit(solution)/shard_map/own_attention/pallas_call | solution.py:341
  124.6 0.3 all-to-all-done.5.final_ref
  124.9 0.9 copy-done.2
  125.8 8.2 %finish.1 = (bf16[96,2560]{1,0:T(8,128)(2,1)}, f32[96,2560]{1,0:T(8,128)}) custom-call(s32[1]{0:T(128)} %bitcast.turn_ref.mine_ref, bf16[8,400,128]{2,1,0:T(8,128)(2,1)} %copy-done.2, bf16[2048,2560]{1,0:T(8,128)(2,1)} %weight_ref.1, f32[1536,128]{1,0:T(8,128)} %get-tuple-element.27.refs_0_, f32[1536,128]{1,0:T(8,128)} %get-tuple-element.28.refs_1_, ...), custom_call_target="tpu_custom_call" | custom-call | flops 2013265920 | bytes 10485760 | tf_op jit(solution)/shard_map/finish/pallas_call | solution.py:422
  134.0 0.1 collective-permute-start
  134.1 2.0 %collective-permute-done = bf16[96,2560]{1,0:T(8,128)(2,1)S(1)} collective-permute-done((bf16[96,2560]{1,0:T(8,128)(2,1)}, bf16[96,2560]{1,0:T(8,128)(2,1)S(1)}, u32[]{:S(2)}, u32[]{:S(2)}) %collective-permute-start) | collective-permute-done | bytes 491552 | tf_op jit(solution)/shard_map/ppermute | solution.py:508
  136.1 1.3 convert_add_fusion
  137.5 1.7 %collective-permute-start.1 = (bf16[48,2560]{1,0:T(8,128)(2,1)S(1)}, bf16[48,2560]{1,0:T(8,128)(2,1)S(1)}, u32[]{:S(2)}, u32[]{:S(2)}) collective-permute-start(bf16[48,2560]{1,0:T(8,128)(2,1)S(1)} %fusion.1), channel_id=1, source_target_pairs={{0,2},{1,3},{2,0},{3,1},{4,6},{5,7},{6,4},{7,5},{8,10},{9,11},{10,... | collective-permute-start | bytes 737288 | tf_op jit(solution)/shard_map/ppermute | solution.py:508
  139.2 6.4 %collective-permute-done.1 = bf16[48,2560]{1,0:T(8,128)(2,1)S(1)} collective-permute-done((bf16[48,2560]{1,0:T(8,128)(2,1)S(1)}, bf16[48,2560]{1,0:T(8,128)(2,1)S(1)}, u32[]{:S(2)}, u32[]{:S(2)}) %collective-permute-start.1) | collective-permute-done | bytes 245792 | tf_op jit(solution)/shard_map/ppermute | solution.py:508
  145.6 0.1 fusion
  145.6 0.8 reshape.82
  (11 shorter events, 0.1 us)
Async XLA Ops:
  9.9 21.3 %all-to-all-start = ((bf16[8,400,128]{2,1,0:T(8,128)(2,1)}), bf16[8,400,128]{2,1,0:T(8,128)(2,1)S(1)}, u32[]{:S(2)}, u32[]{:S(2)}) async-start(bf16[8,400,128]{2,1,0:T(8,128)(2,1)} %pack.1), calls=%async_computation | async-start | bytes 1638400 | tf_op jit(solution)/shard_map/all_to_all | solution.py:480
  17.7 13.4 %copy-start = (f32[8,128]{1,0:T(8,128)S(1)}, f32[8,128]{1,0:T(8,128)}, u32[]{:S(2)}) copy-start(f32[8,128]{1,0:T(8,128)} %get-tuple-element.21.refs_0_) | copy-start | bytes 12292
  32.3 0.7 copy-start.1
  47.7 18.9 %all-to-all-start.1 = ((bf16[8,4,64,128]{3,2,1,0:T(8,128)(2,1)}), bf16[8,4,64,128]{3,2,1,0:T(8,128)(2,1)S(1)}, u32[]{:S(2)}, u32[]{:S(2)}) async-start(bf16[8,4,64,128]{3,2,1,0:T(8,128)(2,1)} %get-tuple-element.23), calls=%async_computation.1 | async-start | bytes 1048576 | tf_op jit(solution)/shard_map/all_to_all | solution.py:480
  66.7 6.0 %copy-start.3 = (bf16[8,4,64,128]{3,2,1,0:T(8,128)(2,1)}, bf16[8,4,64,128]{3,2,1,0:T(8,128)(2,1)S(1)}, u32[]{:S(2)}) copy-start(bf16[8,4,64,128]{3,2,1,0:T(8,128)(2,1)S(1)} %all-to-all-done.1.query_ref) | copy-start | bytes 1572868
  66.7 21.3 %all-to-all-start.4 = ((bf16[8,272,128]{2,1,0:T(8,128)(2,1)}), bf16[8,272,128]{2,1,0:T(8,128)(2,1)S(1)}, u32[]{:S(2)}, u32[]{:S(2)}) async-start(bf16[8,272,128]{2,1,0:T(8,128)(2,1)} %prompt_attention.3), calls=%async_computation.4 | async-start | bytes 1114112 | tf_op jit(solution)/shard_map/all_to_all | solution.py:480
  87.9 22.8 %copy-start.4 = (s32[96]{0:T(128)S(1)}, s32[96]{0:T(128)}, u32[]{:S(2)}) copy-start(s32[96]{0:T(128)} %param.14) | copy-start | bytes 1156
  107.2 17.6 %all-to-all-start.5 = ((bf16[8,400,128]{2,1,0:T(8,128)(2,1)}), bf16[8,400,128]{2,1,0:T(8,128)(2,1)S(1)}, u32[]{:S(2)}, u32[]{:S(2)}) async-start(bf16[8,400,128]{2,1,0:T(8,128)(2,1)} %sort.1.refs_6_), calls=%async_computation.5 | async-start | bytes 1638400 | tf_op jit(solution)/shard_map/all_to_all | solution.py:480
  124.9 0.9 copy-start.2
  134.0 2.1 %collective-permute-start = (bf16[96,2560]{1,0:T(8,128)(2,1)}, bf16[96,2560]{1,0:T(8,128)(2,1)S(1)}, u32[]{:S(2)}, u32[]{:S(2)}) collective-permute-start(bf16[96,2560]{1,0:T(8,128)(2,1)} %get-tuple-element.32), channel_id=1, source_target_pairs={{0,1},{1,0},{2,3},{3,2},{4,5},{5,4},{6,7},{7,6},{8,9},{9,8},{10,11... | collective-permute-start | bytes 1474568 | tf_op jit(solution)/shard_map/ppermute | solution.py:508
  137.5 8.1 %collective-permute-start.1 = (bf16[48,2560]{1,0:T(8,128)(2,1)S(1)}, bf16[48,2560]{1,0:T(8,128)(2,1)S(1)}, u32[]{:S(2)}, u32[]{:S(2)}) collective-permute-start(bf16[48,2560]{1,0:T(8,128)(2,1)S(1)} %fusion.1), channel_id=1, source_target_pairs={{0,2},{1,3},{2,0},{3,1},{4,6},{5,7},{6,4},{7,5},{8,10},{9,11},{10,... | collective-permute-start | bytes 737288 | tf_op jit(solution)/shard_map/ppermute | solution.py:508
